TPU v7x, 512 devices: a whole 4x8x8 slice. The times are simulated.
512 devices in a mesh: dp: 32 (over y_lo, z), tensor: 16 (over x, y_hi, core).
Axes of the slice: x: 4, y: 8 (y_hi: 2, y_lo: 4; y = y_hi * 4 + y_lo), z: 8, core: 2. Of those that a mesh axis runs over, the one named last changes fastest.
Arguments:
- q_latent: bfloat16 [32768, 1536], P(('dp', 'tensor')), parts along dimension 0, may hold values from -150 to 150
- kv_latent: bfloat16 [32768, 576], P(('dp', 'tensor')), parts along dimension 0, may hold values from -700 to 700
- q_gain: float32 [1536], replicated, may hold values from 0.1 to 1.9
- kv_gain: float32 [512], replicated, may hold values from 0.1 to 1.9
- w_q_up: bfloat16 [1536, 12288], P(None, 'tensor'), may hold values from -0.25 to 0.25
- w_kv_up: bfloat16 [512, 16384], P(None, 'tensor'), may hold values from -0.4375 to 0.4375
Outputs:
- attended: bfloat16 [32768, 8192], P(('dp', 'tensor')), parts along dimension 0
There are 32 independent parts, one for each index of `dp`. A program takes and returns all parts, laid end to end along the dimension named above; an argument that names none is the same for every part. Nothing has to cross between parts.
All inputs are finite; a program needn't handle non-finite values.
Results may differ from a plain program's by a relative error of at most 0.03.
Values may be sent and summed in bfloat16 or wider, within the bound.
A program may use at most 64 MiB of HBM per device.

v0:
```python
import jax
import jax.numpy as jnp
from jax import lax
from jax.sharding import PartitionSpec as P

ROPE = 64
NOPE = 128
VDIM = 128


EPSILON = 1e-06


def normalize(latent, gain_vector):
    widened = latent.astype(jnp.float32)
    mean_square = jnp.mean(widened * widened, axis=-1, keepdims=True)
    return (widened * lax.rsqrt(mean_square + EPSILON) * gain_vector).astype(jnp.bfloat16)


def angle_tables(positions, width):
    half_width = width // 2
    exponent = jnp.arange(half_width, dtype=jnp.float32) * (2.0 / width)
    frequency = jnp.power(10000.0, -exponent)
    angles = positions[:, None] * frequency[None, :]
    return (jnp.cos(angles), jnp.sin(angles))


def rotate(vectors, cosine_table, sine_table):
    half_width = vectors.shape[-1] // 2
    first_half = vectors[..., :half_width]
    second_half = vectors[..., half_width:]
    return jnp.concatenate(
        [
            first_half * cosine_table - second_half * sine_table,
            second_half * cosine_table + first_half * sine_table,
        ],
        axis=-1,
    )


def attend(queries, keys_values, key_rope, head_count):
    length = queries.shape[0]
    block_count = max(1, length // 512)
    block_rows = length // block_count
    score_scale = (NOPE + ROPE) ** (-0.5)
    outputs = []
    for block in range(block_count):
        first_row = block * block_rows
        last_row = first_row + block_rows
        query_block = queries[first_row:last_row]
        key_block = keys_values[:last_row]
        scores = jnp.einsum(
            "qhd,khd->hqk",
            query_block[..., :NOPE],
            key_block[..., :NOPE],
            preferred_element_type=jnp.float32,
        )
        scores = scores + jnp.einsum(
            "qhd,kd->hqk",
            query_block[..., NOPE:],
            key_rope[:last_row],
            preferred_element_type=jnp.float32,
        )
        causal = (first_row + jnp.arange(block_rows))[:, None] >= jnp.arange(last_row)[None, :]
        scores = jnp.where(causal[None], scores * score_scale, -jnp.inf)
        weights = jax.nn.softmax(scores, axis=-1).astype(jnp.bfloat16)
        mixed = jnp.einsum(
            "hqk,khd->qhd", weights, key_block[..., NOPE:], preferred_element_type=jnp.float32
        ).astype(jnp.bfloat16)
        outputs.append(mixed.reshape(block_rows, head_count * VDIM))
    return jnp.concatenate(outputs, axis=0)


def shards(q_latent, kv_latent, q_gain, kv_gain, w_q_up, w_kv_up):
    local_rows = q_latent.shape[0]
    latent_width = kv_gain.shape[0]
    head_count = w_q_up.shape[1] // (NOPE + ROPE)
    own_first = lax.axis_index("tensor") * local_rows
    q_send = normalize(q_latent, q_gain)
    row_count = kv_latent.shape[0]
    positions = (own_first + jnp.arange(row_count)).astype(jnp.float32)
    cosine_table, sine_table = angle_tables(positions, ROPE)
    rotary = rotate(kv_latent[:, latent_width:].astype(jnp.float32), cosine_table, sine_table)
    kv_send = jnp.concatenate(
        [normalize(kv_latent[:, :latent_width], kv_gain), rotary.astype(jnp.bfloat16)], axis=1
    )
    q_whole, kv_whole = (
        lax.all_gather(q_send, "tensor", axis=0, tiled=True),
        lax.all_gather(kv_send, "tensor", axis=0, tiled=True),
    )
    row_count = q_whole.shape[0]
    positions = jnp.arange(row_count).astype(jnp.float32)
    cosine_table, sine_table = angle_tables(positions, ROPE)
    projected = jnp.dot(q_whole, w_q_up, preferred_element_type=jnp.float32)
    projected = projected.reshape(row_count, head_count, NOPE + ROPE)
    rotated = jnp.concatenate(
        [
            projected[..., :NOPE],
            rotate(projected[..., NOPE:], cosine_table[:, None, :], sine_table[:, None, :]),
        ],
        axis=-1,
    )
    queries = rotated.astype(jnp.bfloat16).reshape(row_count, head_count * (NOPE + ROPE))
    expanded = jnp.dot(kv_whole[:, :latent_width], w_kv_up, preferred_element_type=jnp.float32)
    keys_joined = jnp.concatenate(
        [expanded.astype(jnp.bfloat16), kv_whole[:, latent_width:]], axis=1
    )
    length = queries.shape[0]
    pair_width = head_count * (NOPE + VDIM)
    attended = attend(
        queries.reshape(length, head_count, NOPE + ROPE),
        keys_joined[:, :pair_width].reshape(length, head_count, NOPE + VDIM),
        keys_joined[:, pair_width:],
        head_count,
    )
    return lax.all_to_all(attended, "tensor", split_axis=0, concat_axis=1, tiled=True)


def solution(mesh):
    return jax.shard_map(
        shards,
        mesh=mesh,
        in_specs=(
            P(("dp", "tensor"), None),
            P(("dp", "tensor"), None),
            P(),
            P(),
            P(None, "tensor"),
            P(None, "tensor"),
        ),
        out_specs=P(("dp", "tensor"), None),
        check_vma=False,
    )
```

profile of v0, /device:TPU:17, one launch (start us, length us, event | category | flops | bytes accessed | tf_op | source)
XLA Modules:
  0.0 242.5 jit_solution(12558046615202617013)
XLA Ops:
  6.5 0.0 copy-start
  6.5 0.0 all-gather.3.cloned.1.call-start
  6.6 0.9 slice.76
  7.4 1.0 fusion.25
  8.4 0.1 copy.59
  8.5 0.1 fusion.33
  8.7 0.1 copy.45
  8.8 0.1 copy.46
  8.9 0.9 fusion.27
  9.8 0.7 pad_maximum_fusion.3
  10.5 0.0 all-gather.3.cloned.1.call-update
  10.6 0.0 all-gather.5.cloned.1.call-start
  10.6 1.1 fusion.18
  11.7 1.7 fusion.20
  13.4 0.0 all-gather.5.cloned.1.call-update
  13.5 0.8 iota_compare_fusion.1
  14.3 1.2 multiply_cosine_fusion
  15.5 1.2 iota_compare_fusion
  16.6 59.5 %all-gather.3.cloned.1.call-done = bf16[1024,576]{1,0:T(8,128)(2,1)} async-done(((bf16[64,576]{1,0:T(8,128)(2,1)}), bf16[1024,576]{1,0:T(8,128)(2,1)}) %all-gather.3.cloned.1.call-update) | async-done | bytes 1179664 | tf_op jit(solution)/shard_map/all_gather | solution.py:89
  76.1 2.8 %convolution_convert_fusion = bf16[1024,1024]{0,1:T(8,128)(2,1)S(1)} fusion(bf16[512,1024]{1,0:T(8,128)(2,1)} %param.11, bf16[1024,576]{1,0:T(8,128)(2,1)} %all-gather.3.cloned.1.call-done), kind=kOutput, calls=%fused_computation.15 | convolution fusion | flops 1074790400 | bytes 4194304 | tf_op jit(solution)/shard_map/dot_general | solution.py:104
  79.0 0.0 copy-start.4
  79.0 1.4 copy-done.4
  80.4 0.1 slice.97
  80.5 0.0 copy-start.3
  80.5 70.5 %all-gather.5.cloned.1.call-done = bf16[1024,1536]{1,0:T(8,128)(2,1)} async-done(((bf16[64,1536]{1,0:T(8,128)(2,1)}), bf16[1024,1536]{1,0:T(8,128)(2,1)}) %all-gather.5.cloned.1.call-update) | async-done | bytes 3145744 | tf_op jit(solution)/shard_map/all_gather | solution.py:88
  150.9 0.0 copy-done
  150.9 6.2 %fusion.42 = f32[1024,768]{0,1:T(8,128)} fusion(bf16[1024,1536]{1,0:T(8,128)(2,1)} %all-gather.5.cloned.1.call-done, bf16[1536,768]{1,0:T(8,128)(2,1)S(1)} %copy-done), kind=kOutput, calls=%fused_computation.73 | convolution fusion | flops 2415919104 | bytes 8650752 | tf_op jit(solution)/shard_map/dot_general | solution.py:94
  157.2 4.4 %copy.47 = bf16[1024,4,192]{2,0,1:T(8,128)(2,1)} copy(f32[1024,4,192]{0,2,1:T(8,128)} %bitcast.40) | data formatting | bytes 4718592 | tf_op jit(solution)/shard_map/reshape | solution.py:95
  161.6 0.0 copy-done.3
  161.6 1.8 fusion.14
  163.4 0.0 copy-done.8
  163.4 1.4 subtract_convert_fusion
  164.8 1.8 fusion.5
  166.6 0.0 copy-start.2
  166.6 1.9 copy-done.2
  168.5 0.8 fusion.41
  169.4 5.6 %fusion.9 = bf16[4,128,512]{2,1,0:T(8,128)(2,1)} fusion(f32[4,512]{1,0:T(4,128)S(1)} %fusion.41, bf16[512,4,256]{0,2,1:T(8,128)(2,1)} %bitcast.45, f32[4,512,512]{1,2,0:T(8,128)} %copy-done.2), kind=kOutput, calls=%fused_computation.17 | convolution fusion | flops 271845888 | bytes 9445376 | tf_op jit(solution)/shard_map/hqk,khd->qhd/dot_general | solution.py:67
  175.0 1.3 copy.54
  176.2 2.4 fusion.23
  178.7 2.9 %fusion.3 = f32[4,512,1024]{2,1,0:T(8,128)S(1)} fusion(f32[1024,512,4]{0,1,2:T(8,128)S(1)} %fusion.23, pred[512,1024]{1,0:T(8,128)(4,1)S(1)} %copy-done.6, bf16[1024,4,256]{0,2,1:T(8,128)(2,1)S(1)} %bitcast.47, bf16[1024,4,192]{2,0,1:T(8,128)(2,1)} %copy.47), kind=kOutput, calls=%fused_computation.4 | convolution fusion | flops 543162368 | bytes 18874368 | tf_op jit(solution)/shard_map/qhd,khd->hqk/dot_general | solution.py:52
  181.6 0.0 copy-start.1
  181.6 3.2 %copy-done.1 = f32[4,512,1024]{2,1,0:T(8,128)} copy-done((f32[4,512,1024]{2,1,0:T(8,128)}, f32[4,512,1024]{2,1,0:T(8,128)S(1)}, u32[]{:S(2)}) %copy-start.1) | copy-done | bytes 8388632
  184.8 2.0 fusion.40
  186.9 10.9 %fusion.8 = bf16[4,128,512]{2,1,0:T(8,128)(2,1)} fusion(f32[4,512]{1,0:T(4,128)S(1)} %fusion.40, bf16[1024,4,256]{0,2,1:T(8,128)(2,1)} %bitcast.46, f32[4,512,1024]{2,1,0:T(8,128)} %copy-done.1), kind=kOutput, calls=%fused_computation.16 | convolution fusion | flops 543427584 | bytes 18358272 | tf_op jit(solution)/shard_map/hqk,khd->qhd/dot_general | solution.py:67
  197.8 1.3 copy.55
  199.0 0.1 pad_maximum_fusion
  199.1 35.5 %all_to_all.19 = bf16[16,64,512]{2,1,0:T(8,128)(2,1)S(1)} all-to-all(bf16[16,64,512]{2,1,0:T(8,128)(2,1)S(1)} %bitcast.42), channel_id=1, replica_groups=mesh['dp'=32,'tensor'=16] {'tensor'}, dimensions={0} | all-to-all | bytes 2097152 | tf_op jit(solution)/shard_map/all_to_all | solution.py:116
  234.6 1.1 copy.64
  (14 shorter events, 0.1 us)
Async XLA Ops:
  6.5 144.4 %copy-start = (bf16[1536,768]{1,0:T(8,128)(2,1)S(1)}, bf16[1536,768]{1,0:T(8,128)(2,1)}, u32[]{:S(2)}) copy-start(bf16[1536,768]{1,0:T(8,128)(2,1)} %param.10) | copy-start | bytes 7077892
  6.5 69.6 %all-gather.3.cloned.1.call-start = ((), (), s32[]{:S(2)}) async-start(), calls=%async_computation.1 | async-start | bytes 1392640 | tf_op jit(solution)/shard_map/all_gather | solution.py:89
  10.6 140.4 %all-gather.5.cloned.1.call-start = ((), (), s32[]{:S(2)}) async-start(), calls=%async_computation.2 | async-start | bytes 3342336 | tf_op jit(solution)/shard_map/all_gather | solution.py:88
  79.0 1.4 copy-start.4
  80.5 81.1 %copy-start.3 = (bf16[512,1024]{0,1:T(8,128)(2,1)}, bf16[512,1024]{0,1:T(8,128)(2,1)S(1)}, u32[]{:S(2)}) copy-start(bf16[512,1024]{0,1:T(8,128)(2,1)S(1)} %slice.97) | copy-start | bytes 3145732
  161.5 1.9 copy-start.8
  161.5 3.2 %copy-start.7 = (pred[512,512]{0,1:T(8,128)(4,1)S(1)}, pred[512,512]{0,1:T(8,128)(4,1)}, u32[]{:S(2)}) copy-start(pred[512,512]{0,1:T(8,128)(4,1)} %iota_compare_fusion.1) | copy-start | bytes 786436
  166.6 1.9 copy-start.2
  176.2 2.4 copy-start.5
  176.2 2.4 copy-start.6
  181.6 3.2 %copy-start.1 = (f32[4,512,1024]{2,1,0:T(8,128)}, f32[4,512,1024]{2,1,0:T(8,128)S(1)}, u32[]{:S(2)}) copy-start(f32[4,512,1024]{2,1,0:T(8,128)S(1)} %fusion.3) | copy-start | bytes 25165828
Sparse Core Ops, SparseCore 0:
  10.7 65.3 all-gather.2
  79.4 71.4 all-gather.4
where the time goes:
time: 243 us; the launch traced here: 242 us
  waiting for transfers between devices  130 us (53%)
  blocking collectives  35.5 us (15%)
  matrix products  34.6 us (14%)
  local copies, waits for them, and re-layouts  15.7 us (6%)
  between operations  13.6 us (6%)
  other arithmetic  13 us (5%)
    all_gather x1, waiting for transfers between devices, shards(): lax.all_gather(q_send, 'tensor', axis=0, tiled=True)  70.5 us
    all_gather x1, waiting for transfers between devices, shards(): lax.all_gather(kv_send, 'tensor', axis=0, tiled=True)  59.5 us
    all_to_all x1, blocking collectives, shards(): lax.all_to_all(attended, 'tensor', split_axis=0, concat_axis=1, tiled=True)  35.5 us
    dot_general x2, matrix products, attend(): jnp.einsum('hqk,khd->qhd', weights, key_block[..., NOPE:], preferred_elem...  16.5 us
    unnamed x19, local copies, waits for them, and re-layouts  6.64 us
    dot_general x1, matrix products, shards(): projected = jnp.dot(q_whole, w_q_up, preferred_element_type=jnp.float32)  6.24 us
  transfers between devices with their start and end apart: 2, of which 2 were waited for; matrix products, arithmetic and copies ran while one was open for 4% of the time, Pallas kernels for 0%

commit v1 on v0

v1 whole, which is shorter than its diff:
```python
import functools

import jax
import jax.numpy as jnp
import numpy as np
from jax import lax
from jax.experimental import pallas as pl
from jax.experimental.pallas import tpu as pltpu
from jax.sharding import PartitionSpec as P

ROPE = 64
NOPE = 128
VDIM = 128
Q_LAT = 1536
KV_LAT = 512
SEQ = 1024
GROUP = 16
ROWS = SEQ // GROUP
HEADS = 4
KV_WIDE = KV_LAT + 2 * ROPE
EPSILON = 1e-06
SCORE_SCALE = (NOPE + ROPE) ** (-0.5) * float(np.log2(np.e))
MESH = pl.DeviceIdType.MESH
KV, Q = 0, 1


def angle_table():
    frequency = 10000.0 ** (-np.arange(ROPE // 2) * (2.0 / ROPE))
    angles = np.arange(SEQ)[:, None] * frequency[None, :]
    cosine, sine = np.cos(angles), np.sin(angles)
    table = np.concatenate([cosine, cosine, sine, sine], axis=1) * SCORE_SCALE
    table = table.reshape(4, 2, 2 * ROWS, 2 * ROPE).transpose(1, 0, 2, 3)
    return table.reshape(2, SEQ // 2, 2 * ROPE).astype(np.float32)


def column_map():
    matrix = np.zeros((2 * (NOPE + ROPE), 512), np.float32)
    half = ROPE // 2
    for head in range(2):
        source, target = head * (NOPE + ROPE), head * 256
        for i in range(NOPE + ROPE):
            matrix[source + i, target + i] = 1.0
        for i in range(half):
            matrix[source + NOPE + half + i, target + NOPE + ROPE + i] = -1.0
            matrix[source + NOPE + i, target + NOPE + ROPE + half + i] = 1.0
    return matrix.astype(jnp.bfloat16)


def receive_slots():
    slots = {}
    for kind in (KV, Q):
        for dx in range(4):
            for dh in range(2):
                for dc in range(2):
                    if (dx, dh, dc) == (0, 0, 0):
                        continue
                    subs = (0, 1) if (dx == 2 and dc == 0) else (None,)
                    for sub in subs:
                        slots[(kind, dx, dh, dc, sub)] = len(slots)
    return slots


SLOTS = receive_slots()


def body(
    q_in, kv_in, q_gain, kv_gain, wq_in, wkv_in, table_in, map_in, out,
    q_raw, kv_raw, wq_raw, wq, wkv, table, cmap, q_all, kv_all, keys, values, outs,
    load_sem, send_sem, recv_sem, out_send, out_recv,
):
    me = lax.axis_index("tensor")
    x, h, c = lax.div(me, 4), lax.rem(lax.div(me, 2), 2), lax.rem(me, 2)

    def place(dx, dh, dc):
        x_ = lax.rem(x + dx, 4)
        h_ = h if dh == 0 else 1 - h
        c_ = c if dc == 0 else 1 - c
        return x_, h_, c_

    def index(dx, dh, dc):
        x_, h_, c_ = place(dx, dh, dc)
        return x_ * 4 + h_ * 2 + c_

    def halved(dx, dh, dc):
        x_, h_, c_ = place(dx, dh, dc)
        return h_ * 8 + x_ * 2 + c_

    def block(kind, rel, sub=None):
        first = (index(*rel) if kind == KV else halved(*rel)) * ROWS
        count = ROWS
        if sub is not None:
            first, count = first + sub * (ROWS // 2), ROWS // 2
        ref = kv_all if kind == KV else q_all
        return ref.at[pl.ds(pl.multiple_of(first, 32), count)]

    sent = []

    def send(kind, rel, to, sub=None):
        there = ((rel[0] - to[0]) % 4, rel[1] ^ to[1], rel[2] ^ to[2])
        ref = block(kind, rel, sub)
        copy = pltpu.make_async_remote_copy(
            src_ref=ref, dst_ref=ref, send_sem=send_sem.at[len(sent)],
            recv_sem=recv_sem.at[SLOTS[(kind, *there, sub)]],
            device_id={"tensor": index(*to)}, device_id_type=MESH,
        )
        copy.start()
        sent.append(copy)

    def arrive(kind, rel, sub=None):
        ref = block(kind, rel, sub)
        pltpu.make_async_remote_copy(
            src_ref=ref, dst_ref=ref, send_sem=send_sem.at[0],
            recv_sem=recv_sem.at[SLOTS[(kind, *rel, sub)]],
            device_id={"tensor": index(0, 0, 1)}, device_id_type=MESH,
        ).wait_recv()

    XP, XM, YP, SIB = (1, 0, 0), (3, 0, 0), (0, 1, 0), (0, 0, 1)

    loads = [
        pltpu.make_async_copy(source, target, load_sem.at[i])
        for i, (source, target) in enumerate(
            [(kv_in, kv_raw), (q_in, q_raw), (table_in, table), (wq_in, wq_raw), (map_in, cmap), (wkv_in, wkv)]
        )
    ]
    for load in loads:
        load.start()

    barrier = pltpu.get_barrier_semaphore()
    for peer in range(1, GROUP):
        pl.semaphore_signal(
            barrier, inc=1,
            device_id={"tensor": index(peer // 4, (peer // 2) % 2, peer % 2)}, device_id_type=MESH,
        )

    loads[0].wait()
    loads[2].wait()
    own_kv = block(KV, (0, 0, 0))
    latent = kv_raw[:, :KV_LAT].astype(jnp.float32)
    mean_square = jnp.mean(latent * latent, axis=-1, keepdims=True)
    own_kv[:, :KV_LAT] = (latent * lax.rsqrt(mean_square + EPSILON) * kv_gain[...]).astype(jnp.bfloat16)
    rotary = kv_raw[:, KV_LAT:].astype(jnp.float32)
    swapped = jnp.concatenate([-rotary[:, ROPE // 2 :], rotary[:, : ROPE // 2]], axis=1)
    own_rows = pl.ds(pl.multiple_of((x * 2 + c) * ROWS, ROWS), ROWS)
    angles = table[h, own_rows, :]
    rotated = (rotary * angles[:, :ROPE] + swapped * angles[:, ROPE:]) * (1.0 / SCORE_SCALE)
    rotated = jnp.concatenate([rotated, rotated], axis=1)
    own_kv[:, KV_LAT:] = rotated.astype(jnp.bfloat16)
    loads[1].wait()
    latent = q_raw[...].astype(jnp.float32)
    mean_square = jnp.mean(latent * latent, axis=-1, keepdims=True)
    own_q = block(Q, (0, 0, 0))
    own_q[...] = (latent * lax.rsqrt(mean_square + EPSILON) * q_gain[...]).astype(jnp.bfloat16)

    pl.semaphore_wait(barrier, GROUP - 1)
    for kind in (KV, Q):
        for to in (YP, XP, XM, SIB):
            send(kind, (0, 0, 0), to)

    for head in range(HEADS):
        values[head, :, VDIM:] = jnp.ones((SEQ, 256 - VDIM), jnp.bfloat16)
    loads[3].wait()
    loads[4].wait()
    loads[5].wait()

    def spread(step, _):
        rows = pl.ds(pl.multiple_of(step * 256, 256), 256)
        for pair in range(2):
            wq[rows, pair * 512 : pair * 512 + 512] = jnp.dot(
                wq_raw[rows, pair * 384 : pair * 384 + 384], cmap[...], preferred_element_type=jnp.float32
            ).astype(jnp.bfloat16)
        return 0

    lax.fori_loop(0, Q_LAT // 256, spread, 0)

    def relay_near(kind, dh):
        arrive(kind, (1, dh, 0))
        send(kind, (1, dh, 0), XM, 0)
        send(kind, (1, dh, 0), SIB)
        arrive(kind, (3, dh, 0))
        send(kind, (3, dh, 0), XP, 1)
        send(kind, (3, dh, 0), SIB)

    def relay_far(kind, dh):
        arrive(kind, (2, dh, 0), 0)
        arrive(kind, (2, dh, 0), 1)
        send(kind, (2, dh, 0), SIB)

    def relay_other(kind):
        arrive(kind, YP)
        for to in (XP, XM, SIB):
            send(kind, YP, to)

    relay_near(KV, 0)
    relay_other(KV)
    relay_far(KV, 0)
    relay_near(KV, 1)
    relay_near(Q, 0)
    relay_far(KV, 1)
    for dh in range(2):
        for dx in range(4):
            arrive(KV, (dx, dh, 1))

    def expand(step, _):
        rows = pl.ds(pl.multiple_of(step * 256, 256), 256)
        for head in range(HEADS):
            pair = jnp.dot(
                kv_all[rows, :KV_LAT], wkv[:, head * 256 : head * 256 + 256], preferred_element_type=jnp.float32
            ).astype(jnp.bfloat16)
            keys[head, rows, :NOPE] = pair[:, :NOPE]
            values[head, rows, :VDIM] = pair[:, NOPE:]
            keys[head, rows, NOPE:] = kv_all[rows, KV_LAT:]
        return 0

    lax.fori_loop(0, SEQ // 256, expand, 0)
    relay_far(Q, 0)
    relay_other(Q)
    relay_near(Q, 1)
    relay_far(Q, 1)

    def attend(dh):
        h_ = h if dh == 0 else 1 - h
        row = lax.broadcasted_iota(jnp.int32, (128, 256), 0)
        column = lax.broadcasted_iota(jnp.int32, (128, 256), 1)
        seen = column <= row + h_ * 128

        def one_head(head, _):
            weights = wq[:, pl.ds(pl.multiple_of(head * 256, 256), 256)]
            latents = q_all[pl.ds(pl.multiple_of(h_ * 512, 512), 512), :]
            projected = jnp.dot(latents, weights, preferred_element_type=jnp.float32)
            queries = jnp.concatenate(
                [projected[:, :NOPE] * SCORE_SCALE, projected[:, NOPE:] * table[h_]], axis=1
            ).astype(jnp.bfloat16)
            columns = pl.ds(pl.multiple_of(head * VDIM, VDIM), VDIM)
            for part in range(4):
                last = 256 * (part + 1)
                scores = lax.dot_general(
                    queries[part * 128 : part * 128 + 128], keys[head, :last, :],
                    (((1,), (1,)), ((), ())), preferred_element_type=jnp.float32,
                )
                edge = jnp.where(seen, scores[:, last - 256 :], -jnp.inf)
                scores = edge if part == 0 else jnp.concatenate([scores[:, : last - 256], edge], axis=1)
                highest = jnp.max(scores, axis=1, keepdims=True)
                terms = jnp.exp2(scores - highest).astype(jnp.bfloat16)
                mixed = jnp.dot(terms, values[head, :last, :], preferred_element_type=jnp.float32)
                mixed = mixed[:, :VDIM] / mixed[:, VDIM:]
                rows = pl.ds(pl.multiple_of(h_ * 512 + part * 128, 128), 128)
                outs[rows, columns] = mixed.astype(jnp.bfloat16)
            for dx in range(4):
                for dc in range(2):
                    if (dx, dh, dc) == (0, 0, 0):
                        continue
                    rows = pl.ds(pl.multiple_of(halved(dx, dh, dc) * ROWS, ROWS), ROWS)
                    pltpu.make_async_remote_copy(
                        src_ref=outs.at[rows, columns],
                        dst_ref=out.at[:, pl.ds(pl.multiple_of(me * HEADS * VDIM + head * VDIM, VDIM), VDIM)],
                        send_sem=out_send, recv_sem=out_recv,
                        device_id={"tensor": index(dx, dh, dc)}, device_id_type=MESH,
                    ).start()
            return 0

        lax.fori_loop(0, HEADS, one_head, 0)

    for dx in range(4):
        arrive(Q, (dx, 1, 1))
    attend(1)
    for dx in range(4):
        arrive(Q, (dx, 0, 1))
    attend(0)

    own = pltpu.make_async_copy(
        outs.at[pl.ds(pl.multiple_of(halved(0, 0, 0) * ROWS, ROWS), ROWS)],
        out.at[:, pl.ds(pl.multiple_of(me * HEADS * VDIM, HEADS * VDIM), HEADS * VDIM)],
        load_sem.at[0],
    )
    own.start()
    for copy in sent:
        copy.wait_send()
    own.wait()
    others = (GROUP - 1) * ROWS
    pltpu.make_async_copy(outs.at[pl.ds(0, others)], outs.at[pl.ds(0, others)], out_send).wait()
    width = (GROUP - 1) * HEADS * VDIM
    pltpu.make_async_copy(out.at[:, pl.ds(0, width)], out.at[:, pl.ds(0, width)], out_recv).wait()


def shards(q_latent, kv_latent, q_gain, kv_gain, w_q_up, w_kv_up):
    hbm = pl.BlockSpec(memory_space=pl.ANY)
    vmem = pl.BlockSpec(memory_space=pltpu.VMEM)
    bf16, f32 = jnp.bfloat16, jnp.float32
    return pl.pallas_call(
        body,
        name="latent_attention",
        out_shape=jax.ShapeDtypeStruct((ROWS, GROUP * HEADS * VDIM), bf16),
        in_specs=[hbm, hbm, vmem, vmem, hbm, hbm, hbm, hbm],
        out_specs=hbm,
        scratch_shapes=[
            pltpu.VMEM((ROWS, Q_LAT), bf16),
            pltpu.VMEM((ROWS, KV_LAT + ROPE), bf16),
            pltpu.VMEM((Q_LAT, HEADS * (NOPE + ROPE)), bf16),
            pltpu.VMEM((Q_LAT, HEADS * 256), bf16),
            pltpu.VMEM((KV_LAT, HEADS * 256), bf16),
            pltpu.VMEM((2, SEQ // 2, 2 * ROPE), f32),
            pltpu.VMEM((2 * (NOPE + ROPE), 512), bf16),
            pltpu.VMEM((SEQ, Q_LAT), bf16),
            pltpu.VMEM((SEQ, KV_WIDE), bf16),
            pltpu.VMEM((HEADS, SEQ, 256), bf16),
            pltpu.VMEM((HEADS, SEQ, 256), bf16),
            pltpu.VMEM((SEQ, HEADS * VDIM), bf16),
            pltpu.SemaphoreType.DMA((6,)),
            pltpu.SemaphoreType.DMA((40,)),
            pltpu.SemaphoreType.DMA((len(SLOTS),)),
            pltpu.SemaphoreType.DMA,
            pltpu.SemaphoreType.DMA,
        ],
        compiler_params=pltpu.CompilerParams(
            collective_id=0, has_side_effects=True, vmem_limit_bytes=48 * 2**20
        ),
    )(
        q_latent, kv_latent, q_gain.reshape(1, Q_LAT), kv_gain.reshape(1, KV_LAT), w_q_up, w_kv_up,
        jnp.asarray(angle_table()), jnp.asarray(column_map()),
    )


def solution(mesh):
    return jax.shard_map(
        shards,
        mesh=mesh,
        in_specs=(
            P(("dp", "tensor"), None),
            P(("dp", "tensor"), None),
            P(),
            P(),
            P(None, "tensor"),
            P(None, "tensor"),
        ),
        out_specs=P(("dp", "tensor"), None),
        check_vma=False,
    )
```

time: 243 us -> 82.8 us (0.34)
  the two profiles are of different devices: /device:TPU:17 before, /device:TPU:1 now
where the time goes in v1:
time: 82.8 us; the launch traced here: 82.4 us
  Pallas kernels  73.3 us (89%)
  local copies, waits for them, and re-layouts  9.09 us (11%)
    pallas_call x1, Pallas kernels, shards(): pl.pallas_call(body, name='latent_attention', out_shape=jax.ShapeDtypeStr...  73.3 us
    unnamed x15, local copies, waits for them, and re-layouts  8.39 us

profile of v1, /device:TPU:1, one launch (start us, length us, event | category | flops | bytes accessed | tf_op | source)
XLA Modules:
  0.0 82.4 jit_solution(16164602736433497550)
XLA Ops:
  0.0 0.7 reshape.6.q_gain
  0.7 0.0 copy-start
  0.7 1.7 %copy-done = bf16[1536,768]{1,0:T(8,128)(2,1)S(1)} copy-done((bf16[1536,768]{1,0:T(8,128)(2,1)S(1)}, bf16[1536,768]{1,0:T(8,128)(2,1)}, u32[]{:S(2)}) %copy-start) | copy-done | bytes 2359320
  2.4 0.0 copy-start.1
  2.4 1.2 %copy-done.1 = bf16[512,1024]{1,0:T(8,128)(2,1)S(1)} copy-done((bf16[512,1024]{1,0:T(8,128)(2,1)S(1)}, bf16[512,1024]{1,0:T(8,128)(2,1)}, u32[]{:S(2)}) %copy-start.1) | copy-done | bytes 1048600
  3.6 0.0 copy-start.2
  3.6 1.0 %copy-done.2 = f32[2,512,128]{2,1,0:T(8,128)S(1)} copy-done((f32[2,512,128]{2,1,0:T(8,128)S(1)}, f32[2,512,128]{2,1,0:T(8,128)}, u32[]{:S(2)}) %copy-start.2) | copy-done | bytes 524312
  4.6 0.0 copy-start.3
  4.6 1.0 %copy-done.3 = bf16[384,512]{1,0:T(8,128)(2,1)S(1)} copy-done((bf16[384,512]{1,0:T(8,128)(2,1)S(1)}, bf16[384,512]{1,0:T(8,128)(2,1)}, u32[]{:S(2)}) %copy-start.3) | copy-done | bytes 393240
  5.6 0.0 copy-start.4
  5.6 0.9 %copy-done.4 = bf16[64,1536]{1,0:T(8,128)(2,1)S(1)} copy-done((bf16[64,1536]{1,0:T(8,128)(2,1)S(1)}, bf16[64,1536]{1,0:T(8,128)(2,1)}, u32[]{:S(2)}) %copy-start.4) | copy-done | bytes 196632
  6.6 0.0 copy-start.5
  6.6 0.9 %copy-done.5 = bf16[64,576]{1,0:T(8,128)(2,1)S(1)} copy-done((bf16[64,576]{1,0:T(8,128)(2,1)S(1)}, bf16[64,576]{1,0:T(8,128)(2,1)}, u32[]{:S(2)}) %copy-start.5) | copy-done | bytes 73752
  7.4 0.0 copy-start.6
  7.4 0.7 copy-done.6
  8.1 73.3 %latent_attention.1 = bf16[64,8192]{1,0:T(8,128)(2,1)S(1)} custom-call(bf16[64,1536]{1,0:T(8,128)(2,1)S(1)} %copy-done.4, bf16[64,576]{1,0:T(8,128)(2,1)S(1)} %copy-done.5, f32[1,1536]{1,0:T(1,128)S(1)} %reshape.6.q_gain, f32[1,512]{1,0:T(1,128)S(1)} %bitcast.1, bf16[1536,768]{1,0:T(8,128)(2,1)S(1)} %copy-done, bf16[512,1024]{1,0:T(8,128)(2,1)S(1)} %copy-done.1, ...), custom_call_target="tpu_custom_call" | custom-call | tf_op jit(solution)/shard_map/latent_attention/pallas_call | solution.py:289
  81.5 1.0 %copy.10 = bf16[64,8192]{1,0:T(8,128)(2,1)} copy(bf16[64,8192]{1,0:T(8,128)(2,1)S(1)} %latent_attention.1) | data formatting | bytes 2097152
Async XLA Ops:
  0.7 1.7 %copy-start = (bf16[1536,768]{1,0:T(8,128)(2,1)S(1)}, bf16[1536,768]{1,0:T(8,128)(2,1)}, u32[]{:S(2)}) copy-start(bf16[1536,768]{1,0:T(8,128)(2,1)} %wq_in.1) | copy-start | bytes 7077892
  2.4 1.2 %copy-start.1 = (bf16[512,1024]{1,0:T(8,128)(2,1)S(1)}, bf16[512,1024]{1,0:T(8,128)(2,1)}, u32[]{:S(2)}) copy-start(bf16[512,1024]{1,0:T(8,128)(2,1)} %wkv_in.1) | copy-start | bytes 3145732
  3.6 1.0 %copy-start.2 = (f32[2,512,128]{2,1,0:T(8,128)S(1)}, f32[2,512,128]{2,1,0:T(8,128)}, u32[]{:S(2)}) copy-start(f32[2,512,128]{2,1,0:T(8,128)} %constant.4.clone.table_in) | copy-start | bytes 1572868
  4.6 1.0 %copy-start.3 = (bf16[384,512]{1,0:T(8,128)(2,1)S(1)}, bf16[384,512]{1,0:T(8,128)(2,1)}, u32[]{:S(2)}) copy-start(bf16[384,512]{1,0:T(8,128)(2,1)} %constant.5.clone.map_in) | copy-start | bytes 1179652
  5.6 0.9 %copy-start.4 = (bf16[64,1536]{1,0:T(8,128)(2,1)S(1)}, bf16[64,1536]{1,0:T(8,128)(2,1)}, u32[]{:S(2)}) copy-start(bf16[64,1536]{1,0:T(8,128)(2,1)} %q_in.1) | copy-start | bytes 589828
  6.6 0.9 %copy-start.5 = (bf16[64,576]{1,0:T(8,128)(2,1)S(1)}, bf16[64,576]{1,0:T(8,128)(2,1)}, u32[]{:S(2)}) copy-start(bf16[64,576]{1,0:T(8,128)(2,1)} %kv_in.1) | copy-start | bytes 221188
  7.4 0.7 copy-start.6
